TPU v7x, 1024 devices: a whole 8x8x8 slice. The times are simulated.
1024 devices in a mesh: tm: 32 (over x_hi, y, core), gx: 8 (over z), gy: 4 (over x_lo).
Axes of the slice: x: 8 (x_hi: 2, x_lo: 4; x = x_hi * 4 + x_lo), y: 8, z: 8, core: 2. Of those that a mesh axis runs over, the one named last changes fastest.
Arguments:
- start_state: float32 [32, 32, 64, 512], P('tm', None, 'gx', 'gy'), may hold values from -6 to 6
- wind_x: float32 [32, 32, 64, 512], P('tm', None, 'gx', 'gy'), may hold values from 0.5 to 0.85
- wind_y: float32 [32, 32, 64, 512], P('tm', None, 'gx', 'gy'), may hold values from 0.03 to 0.09
- diffusivity: float32 [32, 32, 64, 512], P('tm', None, 'gx', 'gy'), may hold values from 0.004 to 0.012
- diff_coef: float32 [32, 64, 512], P(None, 'gx', 'gy'), may hold values from 0.05 to 0.24
- time_weight: float32 [32, 32], replicated, may hold values from -1 to 1
Outputs:
- defect: float32 [32, 32, 64, 512], P('tm', None, 'gx', 'gy')
- mixed_defect: float32 [32, 32, 64, 512], P('tm', None, 'gx', 'gy')
All inputs are finite; a program needn't handle non-finite values.
Results may differ from a plain program's by a relative error of at most 0.00012.
Values sent between devices are 32-bit elements; how exact they have to be, the bound alone decides.
A program may use at most 32 MiB of HBM per device.

v0:
```python
import jax
import jax.numpy as jnp
from jax import lax
from jax.sharding import PartitionSpec as P

SECTIONS = 8
PASSES = 4


def with_halo(shard, sides, width):
    for axis, dim in sides:
        devices, length = (lax.axis_size(axis), shard.shape[dim])
        up = [(i, (i + 1) % devices) for i in range(devices - 1)]
        down = [(j, i) for i, j in up]
        last = lax.slice_in_dim(shard, length - width, length, axis=dim)
        initial = lax.slice_in_dim(shard, 0, width, axis=dim)
        before = lax.ppermute(last, axis, up)
        after = lax.ppermute(initial, axis, down)
        shard = jnp.concatenate([before, shard, after], axis=dim)
    return shard


def passed_along(block, axis, distance):
    devices = range(lax.axis_size(axis))
    route = [(i - distance, i) for i in devices if i - distance in devices]
    return lax.ppermute(block, axis, route)


def advance(padded, wind_east, wind_north, kappa):
    inner = padded[..., 1:-1, 1:-1]
    west = padded[..., :-2, 1:-1]
    east = padded[..., 2:, 1:-1]
    south = padded[..., 1:-1, :-2]
    north = padded[..., 1:-1, 2:]
    return (
        inner
        - wind_east * (inner - west)
        - wind_north * (inner - south)
        + kappa * (west + east + south + north - 4.0 * inner)
    )


def smooth(padded, kappa):
    inner = padded[..., 1:-1, 1:-1]
    west = padded[..., :-2, 1:-1]
    east = padded[..., 2:, 1:-1]
    south = padded[..., 1:-1, :-2]
    north = padded[..., 1:-1, 2:]
    return inner + kappa * (west + east + south + north - 4.0 * inner)


def per_device(start_state, wind_x, wind_y, diffusivity, diff_coef, time_weight):
    state = start_state
    for step in range(SECTIONS):
        padded = with_halo(state, (("gx", 2), ("gy", 3)), 1)
        state = advance(padded, wind_x, wind_y, diffusivity)
    previous = passed_along(state, "tm", 1)
    defect = start_state - previous
    slabs = lax.all_to_all(defect, "tm", split_axis=1, concat_axis=0, tiled=True)
    blend = slabs + jnp.einsum("st,tlxy->slxy", time_weight, slabs, precision=lax.Precision.HIGHEST)
    level_count = slabs.shape[1]
    coef_slab = lax.dynamic_slice_in_dim(
        diff_coef, lax.axis_index("tm") * level_count, level_count, 0
    )[None]
    field = blend
    for step in range(PASSES):
        padded = with_halo(field, (("gx", 2), ("gy", 3)), 1)
        field = smooth(padded, coef_slab)
    mixed_defect = lax.all_to_all(field, "tm", split_axis=0, concat_axis=1, tiled=True)
    return (defect, mixed_defect)


def solution(mesh):
    in_specs = (
        P("tm", None, "gx", "gy"),
        P("tm", None, "gx", "gy"),
        P("tm", None, "gx", "gy"),
        P("tm", None, "gx", "gy"),
        P(None, "gx", "gy"),
        P(),
    )
    out_specs = (P("tm", None, "gx", "gy"), P("tm", None, "gx", "gy"))
    return jax.shard_map(
        per_device, mesh=mesh, in_specs=in_specs, out_specs=out_specs, check_vma=False
    )
```

profile of v0, /device:TPU:1, one launch (start us, length us, event | category | flops | bytes accessed | tf_op | source)
XLA Modules:
  0.0 301.0 jit_solution(5619164539478800427)
XLA Ops:
  1.7 5.7 %collective-permute-start = (f32[1,32,1,128]{3,2,0,1:T(1,128)S(1)}, f32[1,32,1,128]{3,2,0,1:T(1,128)S(1)}, u32[]{:S(2)}, u32[]{:S(2)}) collective-permute-start(f32[1,32,1,128]{3,2,0,1:T(1,128)S(1)} %get-tuple-element.52), channel_id=1, source_target_pairs={{0,4},{4,8},{8,12},{12,16},{16,20},{20,24},{24,28},{1,5},{5,9},{9,... | collective-permute-start | bytes 49160 | tf_op jit(solution)/shard_map/ppermute | solution.py:17
  8.7 4.7 %collective-permute-done.1 = f32[1,32,1,128]{3,2,0,1:T(1,128)S(1)} collective-permute-done((f32[1,32,1,128]{3,2,0,1:T(1,128)S(1)}, f32[1,32,1,128]{3,2,0,1:T(1,128)S(1)}, u32[]{:S(2)}, u32[]{:S(2)}) %collective-permute-start.1) | collective-permute-done | bytes 16416 | tf_op jit(solution)/shard_map/ppermute | solution.py:18
  21.1 3.8 %collective-permute-done.3 = f32[1,32,10,1]{3,2,0,1:T(8,128)S(1)} collective-permute-done((f32[1,32,10,1]{3,2,0,1:T(8,128)S(1)}, f32[1,32,10,1]{3,2,0,1:T(8,128)S(1)}, u32[]{:S(2)}, u32[]{:S(2)}) %collective-permute-start.3) | collective-permute-done | bytes 1312 | tf_op jit(solution)/shard_map/ppermute | solution.py:18
  25.3 4.9 %collective-permute-start.4 = (f32[1,32,1,128]{3,2,0,1:T(1,128)S(1)}, f32[1,32,1,128]{3,2,0,1:T(1,128)S(1)}, u32[]{:S(2)}, u32[]{:S(2)}) collective-permute-start(f32[1,32,1,128]{3,2,0,1:T(1,128)S(1)} %get-tuple-element.50), channel_id=1, source_target_pairs={{0,4},{4,8},{8,12},{12,16},{16,20},{20,24},{24,28},{1,5},{5,9},{9,... | collective-permute-start | bytes 49160 | tf_op jit(solution)/shard_map/ppermute | solution.py:17
  31.5 6.4 %collective-permute-done.5 = f32[1,32,1,128]{3,2,0,1:T(1,128)S(1)} collective-permute-done((f32[1,32,1,128]{3,2,0,1:T(1,128)S(1)}, f32[1,32,1,128]{3,2,0,1:T(1,128)S(1)}, u32[]{:S(2)}, u32[]{:S(2)}) %collective-permute-start.5) | collective-permute-done | bytes 16416 | tf_op jit(solution)/shard_map/ppermute | solution.py:18
  44.5 3.8 %collective-permute-done.7 = f32[1,32,10,1]{3,2,0,1:T(8,128)S(1)} collective-permute-done((f32[1,32,10,1]{3,2,0,1:T(8,128)S(1)}, f32[1,32,10,1]{3,2,0,1:T(8,128)S(1)}, u32[]{:S(2)}, u32[]{:S(2)}) %collective-permute-start.7) | collective-permute-done | bytes 1312 | tf_op jit(solution)/shard_map/ppermute | solution.py:18
  48.6 4.1 %collective-permute-start.8 = (f32[1,32,1,128]{3,2,0,1:T(1,128)S(1)}, f32[1,32,1,128]{3,2,0,1:T(1,128)S(1)}, u32[]{:S(2)}, u32[]{:S(2)}) collective-permute-start(f32[1,32,1,128]{3,2,0,1:T(1,128)S(1)} %get-tuple-element.48), channel_id=1, source_target_pairs={{0,4},{4,8},{8,12},{12,16},{16,20},{20,24},{24,28},{1,5},{5,9},{9,... | collective-permute-start | bytes 49160 | tf_op jit(solution)/shard_map/ppermute | solution.py:17
  54.1 3.7 %collective-permute-done.9 = f32[1,32,1,128]{3,2,0,1:T(1,128)S(1)} collective-permute-done((f32[1,32,1,128]{3,2,0,1:T(1,128)S(1)}, f32[1,32,1,128]{3,2,0,1:T(1,128)S(1)}, u32[]{:S(2)}, u32[]{:S(2)}) %collective-permute-start.9) | collective-permute-done | bytes 16416 | tf_op jit(solution)/shard_map/ppermute | solution.py:18
  64.7 3.8 %collective-permute-done.11 = f32[1,32,10,1]{3,2,0,1:T(8,128)S(1)} collective-permute-done((f32[1,32,10,1]{3,2,0,1:T(8,128)S(1)}, f32[1,32,10,1]{3,2,0,1:T(8,128)S(1)}, u32[]{:S(2)}, u32[]{:S(2)}) %collective-permute-start.11) | collective-permute-done | bytes 1312 | tf_op jit(solution)/shard_map/ppermute | solution.py:18
  68.8 4.6 %collective-permute-start.12 = (f32[1,32,1,128]{3,2,0,1:T(1,128)S(1)}, f32[1,32,1,128]{3,2,0,1:T(1,128)S(1)}, u32[]{:S(2)}, u32[]{:S(2)}) collective-permute-start(f32[1,32,1,128]{3,2,0,1:T(1,128)S(1)} %get-tuple-element.46), channel_id=1, source_target_pairs={{0,4},{4,8},{8,12},{12,16},{16,20},{20,24},{24,28},{1,5},{5,9},{9,... | collective-permute-start | bytes 49160 | tf_op jit(solution)/shard_map/ppermute | solution.py:17
  83.3 3.8 %collective-permute-done.15 = f32[1,32,10,1]{3,2,0,1:T(8,128)S(1)} collective-permute-done((f32[1,32,10,1]{3,2,0,1:T(8,128)S(1)}, f32[1,32,10,1]{3,2,0,1:T(8,128)S(1)}, u32[]{:S(2)}, u32[]{:S(2)}) %collective-permute-start.15) | collective-permute-done | bytes 1312 | tf_op jit(solution)/shard_map/ppermute | solution.py:18
  87.4 4.0 %collective-permute-start.16 = (f32[1,32,1,128]{3,2,0,1:T(1,128)S(1)}, f32[1,32,1,128]{3,2,0,1:T(1,128)S(1)}, u32[]{:S(2)}, u32[]{:S(2)}) collective-permute-start(f32[1,32,1,128]{3,2,0,1:T(1,128)S(1)} %get-tuple-element.44), channel_id=1, source_target_pairs={{0,4},{4,8},{8,12},{12,16},{16,20},{20,24},{24,28},{1,5},{5,9},{9,... | collective-permute-start | bytes 49160 | tf_op jit(solution)/shard_map/ppermute | solution.py:17
  101.6 3.8 %collective-permute-done.19 = f32[1,32,10,1]{3,2,0,1:T(8,128)S(1)} collective-permute-done((f32[1,32,10,1]{3,2,0,1:T(8,128)S(1)}, f32[1,32,10,1]{3,2,0,1:T(8,128)S(1)}, u32[]{:S(2)}, u32[]{:S(2)}) %collective-permute-start.19) | collective-permute-done | bytes 1312 | tf_op jit(solution)/shard_map/ppermute | solution.py:18
  119.3 3.8 %collective-permute-done.23 = f32[1,32,10,1]{3,2,0,1:T(8,128)S(1)} collective-permute-done((f32[1,32,10,1]{3,2,0,1:T(8,128)S(1)}, f32[1,32,10,1]{3,2,0,1:T(8,128)S(1)}, u32[]{:S(2)}, u32[]{:S(2)}) %collective-permute-start.23) | collective-permute-done | bytes 1312 | tf_op jit(solution)/shard_map/ppermute | solution.py:18
  136.7 4.1 %collective-permute-done.27 = f32[1,32,10,1]{3,2,0,1:T(8,128)S(1)} collective-permute-done((f32[1,32,10,1]{3,2,0,1:T(8,128)S(1)}, f32[1,32,10,1]{3,2,0,1:T(8,128)S(1)}, u32[]{:S(2)}, u32[]{:S(2)}) %collective-permute-start.27) | collective-permute-done | bytes 1312 | tf_op jit(solution)/shard_map/ppermute | solution.py:18
  152.1 4.2 %collective-permute-done.30 = f32[1,32,10,1]{3,2,0,1:T(8,128)S(1)} collective-permute-done((f32[1,32,10,1]{3,2,0,1:T(8,128)S(1)}, f32[1,32,10,1]{3,2,0,1:T(8,128)S(1)}, u32[]{:S(2)}, u32[]{:S(2)}) %collective-permute-start.30) | collective-permute-done | bytes 1312 | tf_op jit(solution)/shard_map/ppermute | solution.py:17
  156.3 3.8 %collective-permute-done.31 = f32[1,32,10,1]{3,2,0,1:T(8,128)S(1)} collective-permute-done((f32[1,32,10,1]{3,2,0,1:T(8,128)S(1)}, f32[1,32,10,1]{3,2,0,1:T(8,128)S(1)}, u32[]{:S(2)}, u32[]{:S(2)}) %collective-permute-start.31) | collective-permute-done | bytes 1312 | tf_op jit(solution)/shard_map/ppermute | solution.py:18
  160.4 24.2 %collective-permute-start.32 = (f32[1,32,8,128]{3,2,0,1:T(8,128)S(1)}, f32[1,32,8,128]{3,2,0,1:T(8,128)S(1)}, u32[]{:S(2)}, u32[]{:S(2)}) collective-permute-start(f32[1,32,8,128]{3,2,0,1:T(8,128)S(1)} %fusion.28), channel_id=1, source_target_pairs={{0,32},{32,64},{64,96},{96,128},{128,160},{160,192},{192,224},{224... | collective-permute-start | bytes 393224 | tf_op jit(solution)/shard_map/ppermute | solution.py:26
  186.6 24.3 %all_to_all.24 = f32[1,32,8,128]{3,2,0,1:T(8,128)S(1)} all-to-all(f32[1,32,8,128]{3,2,0,1:T(8,128)S(1)} %bitcast_subtract_fusion), channel_id=1, replica_groups=mesh['tm'=32,'gx'=8,'gy'=4] {'tm'}, dimensions={1} | all-to-all | bytes 262144 | tf_op jit(solution)/shard_map/all_to_all | solution.py:59
  222.5 3.8 %collective-permute-done.36 = f32[32,1,10,1]{3,0,2,1:T(8,128)S(1)} collective-permute-done((f32[32,1,10,1]{3,0,2,1:T(8,128)S(1)}, f32[32,1,10,1]{3,0,2,1:T(8,128)S(1)}, u32[]{:S(2)}, u32[]{:S(2)}) %collective-permute-start.36) | collective-permute-done | bytes 1312 | tf_op jit(solution)/shard_map/ppermute | solution.py:18
  238.3 3.8 %collective-permute-done.40 = f32[32,1,10,1]{3,0,2,1:T(8,128)S(1)} collective-permute-done((f32[32,1,10,1]{3,0,2,1:T(8,128)S(1)}, f32[32,1,10,1]{3,0,2,1:T(8,128)S(1)}, u32[]{:S(2)}, u32[]{:S(2)}) %collective-permute-start.40) | collective-permute-done | bytes 1312 | tf_op jit(solution)/shard_map/ppermute | solution.py:18
  253.9 3.8 %collective-permute-done.44 = f32[32,1,10,1]{3,0,2,1:T(8,128)S(1)} collective-permute-done((f32[32,1,10,1]{3,0,2,1:T(8,128)S(1)}, f32[32,1,10,1]{3,0,2,1:T(8,128)S(1)}, u32[]{:S(2)}, u32[]{:S(2)}) %collective-permute-start.44) | collective-permute-done | bytes 1312 | tf_op jit(solution)/shard_map/ppermute | solution.py:18
  270.1 3.8 %collective-permute-done.48 = f32[32,1,10,1]{3,0,2,1:T(8,128)S(1)} collective-permute-done((f32[32,1,10,1]{3,0,2,1:T(8,128)S(1)}, f32[32,1,10,1]{3,0,2,1:T(8,128)S(1)}, u32[]{:S(2)}, u32[]{:S(2)}) %collective-permute-start.48) | collective-permute-done | bytes 1312 | tf_op jit(solution)/shard_map/ppermute | solution.py:18
  274.2 26.2 %all_to_all.25 = f32[32,1,8,128]{3,2,1,0:T(8,128)S(1)} all-to-all(f32[32,1,8,128]{3,2,1,0:T(8,128)S(1)} %copy.79), channel_id=1, replica_groups=mesh['tm'=32,'gx'=8,'gy'=4] {'tm'}, dimensions={0} | all-to-all | bytes 262144 | tf_op jit(solution)/shard_map/all_to_all | solution.py:69
  (143 shorter events, 136.2 us)
Async XLA Ops:
  1.7 7.0 %collective-permute-start = (f32[1,32,1,128]{3,2,0,1:T(1,128)S(1)}, f32[1,32,1,128]{3,2,0,1:T(1,128)S(1)}, u32[]{:S(2)}, u32[]{:S(2)}) collective-permute-start(f32[1,32,1,128]{3,2,0,1:T(1,128)S(1)} %get-tuple-element.52), channel_id=1, source_target_pairs={{0,4},{4,8},{8,12},{12,16},{16,20},{20,24},{24,28},{1,5},{5,9},{9,... | collective-permute-start | bytes 49160 | tf_op jit(solution)/shard_map/ppermute | solution.py:17
  7.4 6.0 %collective-permute-start.1 = (f32[1,32,1,128]{3,2,0,1:T(1,128)S(1)}, f32[1,32,1,128]{3,2,0,1:T(1,128)S(1)}, u32[]{:S(2)}, u32[]{:S(2)}) collective-permute-start(f32[1,32,1,128]{3,2,0,1:T(1,128)S(1)} %get-tuple-element.53), channel_id=1, source_target_pairs={{4,0},{8,4},{12,8},{16,12},{20,16},{24,20},{28,24},{5,1},{9,5},{13... | collective-permute-start | bytes 49160 | tf_op jit(solution)/shard_map/ppermute | solution.py:18
  14.6 6.6 %collective-permute-start.2 = (f32[1,32,10,1]{3,2,0,1:T(8,128)S(1)}, f32[1,32,10,1]{3,2,0,1:T(8,128)S(1)}, u32[]{:S(2)}, u32[]{:S(2)}) collective-permute-start(f32[1,32,10,1]{3,2,0,1:T(8,128)S(1)} %get-tuple-element.20), channel_id=1, source_target_pairs={{0,1},{1,2},{2,3},{4,5},{5,6},{6,7},{8,9},{9,10},{10,11},{12,13},{... | collective-permute-start | bytes 3848 | tf_op jit(solution)/shard_map/ppermute | solution.py:17
  17.9 7.1 %collective-permute-start.3 = (f32[1,32,10,1]{3,2,0,1:T(8,128)S(1)}, f32[1,32,10,1]{3,2,0,1:T(8,128)S(1)}, u32[]{:S(2)}, u32[]{:S(2)}) collective-permute-start(f32[1,32,10,1]{3,2,0,1:T(8,128)S(1)} %get-tuple-element.21), channel_id=1, source_target_pairs={{1,0},{2,1},{3,2},{5,4},{6,5},{7,6},{9,8},{10,9},{11,10},{13,12},{... | collective-permute-start | bytes 3848 | tf_op jit(solution)/shard_map/ppermute | solution.py:18
  25.3 6.2 %collective-permute-start.4 = (f32[1,32,1,128]{3,2,0,1:T(1,128)S(1)}, f32[1,32,1,128]{3,2,0,1:T(1,128)S(1)}, u32[]{:S(2)}, u32[]{:S(2)}) collective-permute-start(f32[1,32,1,128]{3,2,0,1:T(1,128)S(1)} %get-tuple-element.50), channel_id=1, source_target_pairs={{0,4},{4,8},{8,12},{12,16},{16,20},{20,24},{24,28},{1,5},{5,9},{9,... | collective-permute-start | bytes 49160 | tf_op jit(solution)/shard_map/ppermute | solution.py:17
  30.2 7.7 %collective-permute-start.5 = (f32[1,32,1,128]{3,2,0,1:T(1,128)S(1)}, f32[1,32,1,128]{3,2,0,1:T(1,128)S(1)}, u32[]{:S(2)}, u32[]{:S(2)}) collective-permute-start(f32[1,32,1,128]{3,2,0,1:T(1,128)S(1)} %get-tuple-element.51), channel_id=1, source_target_pairs={{4,0},{8,4},{12,8},{16,12},{20,16},{24,20},{28,24},{5,1},{9,5},{13... | collective-permute-start | bytes 49160 | tf_op jit(solution)/shard_map/ppermute | solution.py:18
  38.1 6.4 %collective-permute-start.6 = (f32[1,32,10,1]{3,2,0,1:T(8,128)S(1)}, f32[1,32,10,1]{3,2,0,1:T(8,128)S(1)}, u32[]{:S(2)}, u32[]{:S(2)}) collective-permute-start(f32[1,32,10,1]{3,2,0,1:T(8,128)S(1)} %get-tuple-element.18), channel_id=1, source_target_pairs={{0,1},{1,2},{2,3},{4,5},{5,6},{6,7},{8,9},{9,10},{10,11},{12,13},{... | collective-permute-start | bytes 3848 | tf_op jit(solution)/shard_map/ppermute | solution.py:17
  41.2 7.1 %collective-permute-start.7 = (f32[1,32,10,1]{3,2,0,1:T(8,128)S(1)}, f32[1,32,10,1]{3,2,0,1:T(8,128)S(1)}, u32[]{:S(2)}, u32[]{:S(2)}) collective-permute-start(f32[1,32,10,1]{3,2,0,1:T(8,128)S(1)} %get-tuple-element.19), channel_id=1, source_target_pairs={{1,0},{2,1},{3,2},{5,4},{6,5},{7,6},{9,8},{10,9},{11,10},{13,12},{... | collective-permute-start | bytes 3848 | tf_op jit(solution)/shard_map/ppermute | solution.py:18
  48.6 5.4 %collective-permute-start.8 = (f32[1,32,1,128]{3,2,0,1:T(1,128)S(1)}, f32[1,32,1,128]{3,2,0,1:T(1,128)S(1)}, u32[]{:S(2)}, u32[]{:S(2)}) collective-permute-start(f32[1,32,1,128]{3,2,0,1:T(1,128)S(1)} %get-tuple-element.48), channel_id=1, source_target_pairs={{0,4},{4,8},{8,12},{12,16},{16,20},{20,24},{24,28},{1,5},{5,9},{9,... | collective-permute-start | bytes 49160 | tf_op jit(solution)/shard_map/ppermute | solution.py:17
  58.0 6.7 %collective-permute-start.10 = (f32[1,32,10,1]{3,2,0,1:T(8,128)S(1)}, f32[1,32,10,1]{3,2,0,1:T(8,128)S(1)}, u32[]{:S(2)}, u32[]{:S(2)}) collective-permute-start(f32[1,32,10,1]{3,2,0,1:T(8,128)S(1)} %get-tuple-element.16), channel_id=1, source_target_pairs={{0,1},{1,2},{2,3},{4,5},{5,6},{6,7},{8,9},{9,10},{10,11},{12,13},{... | collective-permute-start | bytes 3848 | tf_op jit(solution)/shard_map/ppermute | solution.py:17
  61.4 7.1 %collective-permute-start.11 = (f32[1,32,10,1]{3,2,0,1:T(8,128)S(1)}, f32[1,32,10,1]{3,2,0,1:T(8,128)S(1)}, u32[]{:S(2)}, u32[]{:S(2)}) collective-permute-start(f32[1,32,10,1]{3,2,0,1:T(8,128)S(1)} %get-tuple-element.17), channel_id=1, source_target_pairs={{1,0},{2,1},{3,2},{5,4},{6,5},{7,6},{9,8},{10,9},{11,10},{13,12},{... | collective-permute-start | bytes 3848 | tf_op jit(solution)/shard_map/ppermute | solution.py:18
  68.8 5.9 %collective-permute-start.12 = (f32[1,32,1,128]{3,2,0,1:T(1,128)S(1)}, f32[1,32,1,128]{3,2,0,1:T(1,128)S(1)}, u32[]{:S(2)}, u32[]{:S(2)}) collective-permute-start(f32[1,32,1,128]{3,2,0,1:T(1,128)S(1)} %get-tuple-element.46), channel_id=1, source_target_pairs={{0,4},{4,8},{8,12},{12,16},{16,20},{20,24},{24,28},{1,5},{5,9},{9,... | collective-permute-start | bytes 49160 | tf_op jit(solution)/shard_map/ppermute | solution.py:17
  80.0 7.1 %collective-permute-start.15 = (f32[1,32,10,1]{3,2,0,1:T(8,128)S(1)}, f32[1,32,10,1]{3,2,0,1:T(8,128)S(1)}, u32[]{:S(2)}, u32[]{:S(2)}) collective-permute-start(f32[1,32,10,1]{3,2,0,1:T(8,128)S(1)} %get-tuple-element.15), channel_id=1, source_target_pairs={{1,0},{2,1},{3,2},{5,4},{6,5},{7,6},{9,8},{10,9},{11,10},{13,12},{... | collective-permute-start | bytes 3848 | tf_op jit(solution)/shard_map/ppermute | solution.py:18
  98.3 7.1 %collective-permute-start.19 = (f32[1,32,10,1]{3,2,0,1:T(8,128)S(1)}, f32[1,32,10,1]{3,2,0,1:T(8,128)S(1)}, u32[]{:S(2)}, u32[]{:S(2)}) collective-permute-start(f32[1,32,10,1]{3,2,0,1:T(8,128)S(1)} %get-tuple-element.13), channel_id=1, source_target_pairs={{1,0},{2,1},{3,2},{5,4},{6,5},{7,6},{9,8},{10,9},{11,10},{13,12},{... | collective-permute-start | bytes 3848 | tf_op jit(solution)/shard_map/ppermute | solution.py:18
  113.8 5.5 %collective-permute-start.22 = (f32[1,32,10,1]{3,2,0,1:T(8,128)S(1)}, f32[1,32,10,1]{3,2,0,1:T(8,128)S(1)}, u32[]{:S(2)}, u32[]{:S(2)}) collective-permute-start(f32[1,32,10,1]{3,2,0,1:T(8,128)S(1)} %get-tuple-element.10), channel_id=1, source_target_pairs={{0,1},{1,2},{2,3},{4,5},{5,6},{6,7},{8,9},{9,10},{10,11},{12,13},{... | collective-permute-start | bytes 3848 | tf_op jit(solution)/shard_map/ppermute | solution.py:17
  116.0 7.1 %collective-permute-start.23 = (f32[1,32,10,1]{3,2,0,1:T(8,128)S(1)}, f32[1,32,10,1]{3,2,0,1:T(8,128)S(1)}, u32[]{:S(2)}, u32[]{:S(2)}) collective-permute-start(f32[1,32,10,1]{3,2,0,1:T(8,128)S(1)} %get-tuple-element.11), channel_id=1, source_target_pairs={{1,0},{2,1},{3,2},{5,4},{6,5},{7,6},{9,8},{10,9},{11,10},{13,12},{... | collective-permute-start | bytes 3848 | tf_op jit(solution)/shard_map/ppermute | solution.py:18
  133.4 7.5 %collective-permute-start.27 = (f32[1,32,10,1]{3,2,0,1:T(8,128)S(1)}, f32[1,32,10,1]{3,2,0,1:T(8,128)S(1)}, u32[]{:S(2)}, u32[]{:S(2)}) collective-permute-start(f32[1,32,10,1]{3,2,0,1:T(8,128)S(1)} %get-tuple-element.9), channel_id=1, source_target_pairs={{1,0},{2,1},{3,2},{5,4},{6,5},{7,6},{9,8},{10,9},{11,10},{13,12},{... | collective-permute-start | bytes 3848 | tf_op jit(solution)/shard_map/ppermute | solution.py:18
  149.2 7.1 %collective-permute-start.30 = (f32[1,32,10,1]{3,2,0,1:T(8,128)S(1)}, f32[1,32,10,1]{3,2,0,1:T(8,128)S(1)}, u32[]{:S(2)}, u32[]{:S(2)}) collective-permute-start(f32[1,32,10,1]{3,2,0,1:T(8,128)S(1)} %get-tuple-element.6), channel_id=1, source_target_pairs={{0,1},{1,2},{2,3},{4,5},{5,6},{6,7},{8,9},{9,10},{10,11},{12,13},{... | collective-permute-start | bytes 3848 | tf_op jit(solution)/shard_map/ppermute | solution.py:17
  150.8 9.3 %collective-permute-start.31 = (f32[1,32,10,1]{3,2,0,1:T(8,128)S(1)}, f32[1,32,10,1]{3,2,0,1:T(8,128)S(1)}, u32[]{:S(2)}, u32[]{:S(2)}) collective-permute-start(f32[1,32,10,1]{3,2,0,1:T(8,128)S(1)} %get-tuple-element.7), channel_id=1, source_target_pairs={{1,0},{2,1},{3,2},{5,4},{6,5},{7,6},{9,8},{10,9},{11,10},{13,12},{... | collective-permute-start | bytes 3848 | tf_op jit(solution)/shard_map/ppermute | solution.py:18
  160.4 26.1 %collective-permute-start.32 = (f32[1,32,8,128]{3,2,0,1:T(8,128)S(1)}, f32[1,32,8,128]{3,2,0,1:T(8,128)S(1)}, u32[]{:S(2)}, u32[]{:S(2)}) collective-permute-start(f32[1,32,8,128]{3,2,0,1:T(8,128)S(1)} %fusion.28), channel_id=1, source_target_pairs={{0,32},{32,64},{64,96},{96,128},{128,160},{160,192},{192,224},{224... | collective-permute-start | bytes 393224 | tf_op jit(solution)/shard_map/ppermute | solution.py:26
  220.3 6.1 %collective-permute-start.36 = (f32[32,1,10,1]{3,0,2,1:T(8,128)S(1)}, f32[32,1,10,1]{3,0,2,1:T(8,128)S(1)}, u32[]{:S(2)}, u32[]{:S(2)}) collective-permute-start(f32[32,1,10,1]{3,0,2,1:T(8,128)S(1)} %get-tuple-element.29), channel_id=1, source_target_pairs={{1,0},{2,1},{3,2},{5,4},{6,5},{7,6},{9,8},{10,9},{11,10},{13,12},{... | collective-permute-start | bytes 3848 | tf_op jit(solution)/shard_map/ppermute | solution.py:18
  236.0 6.1 %collective-permute-start.40 = (f32[32,1,10,1]{3,0,2,1:T(8,128)S(1)}, f32[32,1,10,1]{3,0,2,1:T(8,128)S(1)}, u32[]{:S(2)}, u32[]{:S(2)}) collective-permute-start(f32[32,1,10,1]{3,0,2,1:T(8,128)S(1)} %get-tuple-element.27), channel_id=1, source_target_pairs={{1,0},{2,1},{3,2},{5,4},{6,5},{7,6},{9,8},{10,9},{11,10},{13,12},{... | collective-permute-start | bytes 3848 | tf_op jit(solution)/shard_map/ppermute | solution.py:18
  251.7 6.1 %collective-permute-start.44 = (f32[32,1,10,1]{3,0,2,1:T(8,128)S(1)}, f32[32,1,10,1]{3,0,2,1:T(8,128)S(1)}, u32[]{:S(2)}, u32[]{:S(2)}) collective-permute-start(f32[32,1,10,1]{3,0,2,1:T(8,128)S(1)} %get-tuple-element.25), channel_id=1, source_target_pairs={{1,0},{2,1},{3,2},{5,4},{6,5},{7,6},{9,8},{10,9},{11,10},{13,12},{... | collective-permute-start | bytes 3848 | tf_op jit(solution)/shard_map/ppermute | solution.py:18
  267.9 6.1 %collective-permute-start.48 = (f32[32,1,10,1]{3,0,2,1:T(8,128)S(1)}, f32[32,1,10,1]{3,0,2,1:T(8,128)S(1)}, u32[]{:S(2)}, u32[]{:S(2)}) collective-permute-start(f32[32,1,10,1]{3,0,2,1:T(8,128)S(1)} %get-tuple-element.23), channel_id=1, source_target_pairs={{1,0},{2,1},{3,2},{5,4},{6,5},{7,6},{9,8},{10,9},{11,10},{13,12},{... | collective-permute-start | bytes 3848 | tf_op jit(solution)/shard_map/ppermute | solution.py:18
  (32 other events, 426.3 us)
where the time goes:
time: 303 us; the launch traced here: 301 us
  starting transfers between devices  127 us (42%)
  waiting for transfers between devices  114 us (38%)
  blocking collectives  50.5 us (17%)
  other arithmetic  4.04 us (1%)
  local copies, waits for them, and re-layouts  3.43 us (1%)
    ppermute x24, waiting for transfers between devices, with_halo(): after = lax.ppermute(initial, axis, down)  90.5 us
    ppermute x24, starting transfers between devices, with_halo(): before = lax.ppermute(last, axis, up)  71.7 us
    ppermute x24, starting transfers between devices, with_halo(): after = lax.ppermute(initial, axis, down)  31 us
    all_to_all x1, blocking collectives, per_device(): lax.all_to_all(field, 'tm', split_axis=0, concat_axis=1, tiled=True)  26.2 us
    all_to_all x1, blocking collectives, per_device(): lax.all_to_all(defect, 'tm', split_axis=1, concat_axis=0, tiled=True)  24.3 us
    ppermute x1, starting transfers between devices, passed_along(): return lax.ppermute(block, axis, route)  24.2 us
    ppermute x24, waiting for transfers between devices, with_halo(): before = lax.ppermute(last, axis, up)  21.9 us
  transfers between devices with their start and end apart: 49, of which 37 were waited for; matrix products, arithmetic and copies ran while one was open for 0% of the time, Pallas kernels for 0%

commit v1 on v0

v1 whole, which is shorter than its diff:
```python
import functools

import jax
import jax.numpy as jnp
from jax import lax
from jax.experimental import pallas as pl
from jax.experimental.pallas import tpu as pltpu
from jax.sharding import PartitionSpec as P

MESH = pl.DeviceIdType.MESH

LEV = 32
OWN0, OWN1, ROWS = 16, 144, 160
CHUNK = 16
STATE, B, D, K, C = range(5)
DIRS = ((-1, 0), (1, 0), (-1, -1), (-1, 1), (1, -1), (1, 1), (0, -1), (0, 1))


def rolled(v, shift):
    return pltpu.roll(v, shift % 128, 1)


def stencil(src, dst, coefs, first, last, diffuse, held=1):
    lane = lax.broadcasted_iota(jnp.int32, (CHUNK, 128), 1)
    low, high = lane < 32, lane >= 96
    lowest, highest = max(first - 1, held), min(last + 1, 5 - held)

    def body(i, carry):
        row = pl.multiple_of(8 + i * CHUNK, 8)
        here = pl.ds(row, CHUNK)
        v = {p: src[p, here, :] for p in range(lowest, highest + 1)}
        up = {p: rolled(v[p], 32) for p in range(lowest, last + 1)}
        down = {p: rolled(v[p], -32) for p in range(first, highest + 1)}
        for p in range(first, last + 1):
            west = jnp.where(low, up[p - 1], up[p]) if p > lowest else up[p]
            east = jnp.where(high, down[p + 1], down[p]) if p < highest else down[p]
            south = src[p, pl.ds(row - 1, CHUNK), :]
            north = src[p, pl.ds(row + 1, CHUNK), :]
            mid = v[p]
            if diffuse:
                new = mid + coefs[C, p, here, :] * (((west + east) + (south + north)) - 4.0 * mid)
            else:
                new = (
                    mid
                    + coefs[B, p, here, :] * (west - mid)
                    + coefs[D, p, here, :] * (south - mid)
                    + coefs[K, p, here, :] * ((east + north) - (mid + mid))
                )
            dst[p, here, :] = new
        return carry

    lax.fori_loop(0, (ROWS - 16) // CHUNK, body, 0)


def kernel(
    st_hbm, wx_hbm, wy_hbm, kf_hbm, dc_hbm, tw_ref,
    defect_ref, mixed_ref,
    raw, ext, second, ping, pong, rows_s, rows_e, rows_o, rows_n, got_s, got_e, prev, dtmp, fin,
    load_sem, send1, recv1, send2, recv2, send3, recv3,
    a2a_send, a2a_recv, next_send, next_recv, out_sem, all_in,
):
    tm, gx, gy = lax.axis_index("tm"), lax.axis_index("gx"), lax.axis_index("gy")
    ntm, ngx, ngy = lax.axis_size("tm"), lax.axis_size("gx"), lax.axis_size("gy")

    def there(dx, dy):
        ok = None
        for cond in (
            (gx > 0) if dx < 0 else None,
            (gx < ngx - 1) if dx > 0 else None,
            (gy > 0) if dy < 0 else None,
            (gy < ngy - 1) if dy > 0 else None,
        ):
            if cond is not None:
                ok = cond if ok is None else jnp.logical_and(ok, cond)
        return ok

    def neighbour(dx, dy):
        return {"gx": gx + dx, "gy": gy + dy}

    barrier = pltpu.get_barrier_semaphore()
    for dx, dy in DIRS:
        @pl.when(there(dx, dy))
        def _(dx=dx, dy=dy):
            pl.semaphore_signal(barrier, 1, device_id=neighbour(dx, dy), device_id_type=MESH)

    @pl.when(tm > 0)
    def _():
        pl.semaphore_signal(barrier, 1, device_id={"tm": 0}, device_id_type=MESH)

    loads = [
        pltpu.make_async_copy(src, raw.at[i], load_sem.at[i])
        for i, src in enumerate((st_hbm.at[0], wx_hbm.at[0], wy_hbm.at[0], kf_hbm.at[0], dc_hbm))
    ]
    for load in loads:
        load.start()

    for ref in (ext.at[STATE], second, ping, pong):
        for p in range(6):
            ref[p, 0:8, :] = jnp.zeros((8, 128), jnp.float32)
            ref[p, ROWS - 8 : ROWS, :] = jnp.zeros((8, 128), jnp.float32)
    fields = [ext.at[i] for i in range(5)] + [second]
    for cond, planes in ((gx == 0, (0, 1)), (gx == ngx - 1, (4, 5))):
        @pl.when(cond)
        def _(planes=planes):
            for ref in fields:
                for p in planes:
                    ref[p] = jnp.zeros((ROWS, 128), jnp.float32)
    for cond, row in ((gy == 0, 8), (gy == ngy - 1, OWN1)):
        @pl.when(cond)
        def _(row=row):
            for ref in fields:
                for p in range(6):
                    ref[p, row : row + 8, :] = jnp.zeros((8, 128), jnp.float32)
    for x in range(8):
        got_e[x, 0:1, :] = jnp.zeros((1, 128), jnp.float32)

    def own_rows(i, half):
        return [raw[i, :, half * 4 + j, :] for j in range(4)]

    def put(i, half, parts):
        ext[i, 2 + half, OWN0:OWN1, :] = jnp.concatenate(parts, axis=0).T

    loads[0].wait()
    for half in range(2):
        put(STATE, half, own_rows(0, half))
    for i in (1, 2, 3):
        loads[i].wait()
    for half in range(2):
        kf = own_rows(3, half)
        put(K, half, kf)
        put(B, half, [a + b for a, b in zip(own_rows(1, half), kf)])
        put(D, half, [a + b for a, b in zip(own_rows(2, half), kf)])
    loads[4].wait()
    for half in range(2):
        put(C, half, own_rows(4, half))

    def y_slices(dy):
        if dy < 0:
            return pl.ds(OWN0, 8), pl.ds(OWN1, 8)
        if dy > 0:
            return pl.ds(OWN1 - 8, 8), pl.ds(OWN0 - 8, 8)
        return pl.ds(OWN0, 128), pl.ds(OWN0, 128)

    def near(dx):
        return (2, 4) if dx < 0 else (3, 1)

    def far(dx):
        return (3, 5) if dx < 0 else (2, 0)

    def copies_first(n, dx, dy):
        ys, yd = y_slices(dy)
        if dx == 0:
            src, dst = ext.at[:, pl.ds(2, 2), ys, :], ext.at[:, pl.ds(2, 2), yd, :]
        else:
            ps, pd = near(dx)
            arrays = pl.ds(0, 4 if dy == 0 else 5)
            src, dst = ext.at[arrays, ps, ys, :], ext.at[arrays, pd, yd, :]
        return [pltpu.make_async_remote_copy(src, dst, send1.at[n], recv1.at[n], device_id=neighbour(dx, dy), device_id_type=MESH)]

    def copies_later(n, dx, dy):
        if dx == 0:
            return []
        ys, yd = y_slices(dy)
        out = []
        if dy == 0:
            ps, pd = near(dx)
            out.append(pltpu.make_async_remote_copy(
                ext.at[C, ps, ys, :], ext.at[C, pd, yd, :], send2.at[6 + n], recv2.at[6 + n], device_id=neighbour(dx, dy), device_id_type=MESH))
        ps, pd = far(dx)
        out.append(pltpu.make_async_remote_copy(
            ext.at[pl.ds(1, 3), ps, ys, :], ext.at[pl.ds(1, 3), pd, yd, :], send2.at[n], recv2.at[n], device_id=neighbour(dx, dy), device_id_type=MESH))
        return out

    def copies_second(n, dx, dy):
        ys, yd = y_slices(dy)
        pd = 2 - 2 * dx
        return [pltpu.make_async_remote_copy(
            second.at[pl.ds(2, 2), ys, :], second.at[pl.ds(pd, 2), yd, :], send3.at[n], recv3.at[n], device_id=neighbour(dx, dy), device_id_type=MESH)]

    def each(copies, act, opposite=False):
        for n, (dx, dy) in enumerate(DIRS):
            sx, sy = (-dx, -dy) if opposite else (dx, dy)

            @pl.when(there(sx, sy))
            def _(n=n, dx=dx, dy=dy):
                for copy in copies(n, dx, dy):
                    act(copy)

    start = lambda copy: copy.start()
    arrived = lambda copy: copy.wait_recv()
    left = lambda copy: copy.wait_send()

    count = jnp.int32(0)
    for dx, dy in DIRS:
        count = count + jnp.where(there(dx, dy), 1, 0)
    pl.semaphore_wait(barrier, count + jnp.where(tm == 0, ntm - 1, 0))

    each(copies_first, start)
    each(copies_later, start)

    @pl.when(tm == 0)
    def _():
        def tell(i, carry):
            pl.semaphore_signal(all_in, 1, device_id={"tm": i}, device_id_type=MESH)
            return carry

        lax.fori_loop(1, ntm, tell, 0)

    each(copies_first, arrived, opposite=True)

    stencil(ext.at[STATE], ping, ext, 1, 4, False)
    stencil(ping, pong, ext, 1, 4, False)
    stencil(pong, ping, ext, 1, 4, False)
    stencil(ping, pong, ext, 2, 3, False)
    for p in (2, 3):
        second[p, OWN0:OWN1, :] = pong[p, OWN0:OWN1, :]
    each(copies_second, start)

    def offset(k):
        dx, j, c = 1 - k // 16, (k // 2) % 8, 1 - k % 2
        dy = jnp.where(j % 2 == 0, 4 + j // 2, 4 - (j + 1) // 2)
        x, y, core = tm // 16, (tm // 2) % 8, tm % 2
        return ((x + dx) % 2) * 16 + ((y + dy) % 8) * 2 + (core + c) % 2

    def exchange(n, src_of, dst_of_me):
        def send(k, carry):
            other = offset(k)
            pltpu.make_async_remote_copy(
                src_of(other), dst_of_me, a2a_send.at[n], a2a_recv.at[n], device_id={"tm": other}, device_id_type=MESH
            ).start()
            return carry

        lax.fori_loop(0, ntm - 1, send, 0)
        pltpu.make_async_copy(src_of(tm), dst_of_me, a2a_recv.at[n]).start()

    def exchanged(n):
        pltpu.make_async_copy(raw.at[1], raw.at[2], a2a_recv.at[n]).wait()

    def sent(n):
        pltpu.make_async_copy(raw.at[1, pl.ds(0, ntm - 1)], raw.at[2, pl.ds(0, ntm - 1)], a2a_send.at[n]).wait()

    def to_rows(planes, dst):
        for half, plane in enumerate(planes):
            flat = plane.T
            for j in range(4):
                dst[half * 4 + j] = flat[j * LEV : (j + 1) * LEV, :]

    each(copies_later, arrived, opposite=True)
    stencil(ext.at[STATE], ping, ext, 1, 4, True)
    stencil(ping, pong, ext, 1, 4, True)
    stencil(pong, ping, ext, 1, 4, True)
    stencil(ping, pong, ext, 2, 3, True)
    to_rows([pong[p, OWN0:OWN1, :] for p in (2, 3)], rows_s)

    @pl.when(tm > 0)
    def _():
        pl.semaphore_wait(all_in, 1)

    exchange(0, lambda t: rows_s.at[:, t, :], got_s.at[:, tm, :])

    each(copies_second, arrived, opposite=True)
    stencil(second, ping, ext, 0, 5, False, 0)
    stencil(ping, pong, ext, 0, 5, False, 0)
    stencil(pong, ping, ext, 0, 5, False, 0)
    stencil(ping, pong, ext, 1, 4, False, 0)
    for p in (2, 3):
        fin[p - 2] = pong[p, OWN0:OWN1, :]
    stencil(pong, ping, ext, 1, 4, True)
    stencil(ping, pong, ext, 1, 4, True)
    stencil(pong, ping, ext, 1, 4, True)
    stencil(ping, pong, ext, 2, 3, True)
    to_rows([pong[p, OWN0:OWN1, :] for p in (2, 3)], rows_e)
    exchange(1, lambda t: rows_e.at[:, t, :], got_e.at[:, tm + 1, :])

    to_rows([fin[0], fin[1]], rows_n)
    onward = pltpu.make_async_remote_copy(
        rows_n, prev, next_send, next_recv, device_id={"tm": jnp.minimum(tm + 1, ntm - 1)}, device_id_type=MESH
    )

    @pl.when(tm < ntm - 1)
    def _():
        onward.start()

    @pl.when(tm == 0)
    def _():
        prev[...] = jnp.zeros_like(prev)

    exchanged(0)
    exchanged(1)
    weights = tw_ref[...]
    for x in range(8):
        both = got_s[x] - got_e[x, 0:LEV, :]
        rows_o[x] = both + jnp.dot(weights, both, precision=lax.Precision.HIGHEST, preferred_element_type=jnp.float32)
    exchange(2, lambda s: rows_o.at[:, s, :], mixed_ref.at[0, tm])

    @pl.when(tm > 0)
    def _():
        onward.wait_recv()

    for x in range(8):
        dtmp[:, x, :] = raw[0, :, x, :] - prev[x]
    store = pltpu.make_async_copy(dtmp, defect_ref.at[0], out_sem)
    store.start()

    each(copies_first, left)
    each(copies_later, left)
    each(copies_second, left)

    @pl.when(tm < ntm - 1)
    def _():
        onward.wait_send()

    sent(0)
    sent(1)
    store.wait()
    exchanged(2)
    sent(2)


def per_device(start_state, wind_x, wind_y, diffusivity, diff_coef, time_weight):
    f32 = jnp.float32
    any_space = pl.BlockSpec(memory_space=pl.ANY)
    dma = pltpu.SemaphoreType.DMA
    return pl.pallas_call(
        kernel,
        out_shape=(jax.ShapeDtypeStruct(start_state.shape, f32),) * 2,
        in_specs=[any_space] * 5 + [pl.BlockSpec(memory_space=pltpu.VMEM)],
        out_specs=(any_space, any_space),
        scratch_shapes=[
            pltpu.VMEM((5, LEV, 8, 128), f32),
            pltpu.VMEM((5, 6, ROWS, 128), f32),
            pltpu.VMEM((6, ROWS, 128), f32),
            pltpu.VMEM((6, ROWS, 128), f32),
            pltpu.VMEM((6, ROWS, 128), f32),
            pltpu.VMEM((8, LEV, 128), f32),
            pltpu.VMEM((8, LEV, 128), f32),
            pltpu.VMEM((8, LEV, 128), f32),
            pltpu.VMEM((8, LEV, 128), f32),
            pltpu.VMEM((8, LEV, 128), f32),
            pltpu.VMEM((8, LEV + 8, 128), f32),
            pltpu.VMEM((8, LEV, 128), f32),
            pltpu.VMEM((LEV, 8, 128), f32),
            pltpu.VMEM((2, 128, 128), f32),
            dma((5,)),
            dma((8,)), dma((8,)), dma((8,)), dma((8,)), dma((8,)), dma((8,)),
            dma((3,)), dma((3,)),
            dma, dma, dma,
            pltpu.SemaphoreType.REGULAR,
        ],
        compiler_params=pltpu.CompilerParams(
            collective_id=0, has_side_effects=True, vmem_limit_bytes=32 * 1024 * 1024
        ),
    )(start_state, wind_x, wind_y, diffusivity, diff_coef, time_weight)


def solution(mesh):
    split = P("tm", None, "gx", "gy")
    return jax.shard_map(
        per_device,
        mesh=mesh,
        in_specs=(split, split, split, split, P(None, "gx", "gy"), P()),
        out_specs=(split, split),
        check_vma=False,
    )
```

time: 303 us -> 61.5 us (0.20)
  the two profiles are of different devices: /device:TPU:1 before, /device:TPU:256 now
where the time goes in v1:
time: 61.5 us; the launch traced here: 61.3 us
  Pallas kernels  54.1 us (88%)
  local copies, waits for them, and re-layouts  6.54 us (11%)
  between operations  0.65 us (1%)
    pallas_call x1, Pallas kernels, per_device(): pl.pallas_call(kernel, out_shape=(jax.ShapeDtypeStruct(start_state.shape,...  54.1 us
    unnamed x14, local copies, waits for them, and re-layouts  6.54 us

profile of v1, /device:TPU:256, one launch (start us, length us, event | category | flops | bytes accessed | tf_op | source)
XLA Modules:
  0.0 61.3 jit_solution(6078035656070676846)
XLA Ops:
  0.6 0.0 copy-start
  0.6 0.9 %copy-done = f32[1,32,8,128]{3,2,1,0:T(8,128)S(1)} copy-done((f32[1,32,8,128]{3,2,1,0:T(8,128)S(1)}, f32[1,32,8,128]{3,2,1,0:T(8,128)}, u32[]{:S(2)}) %copy-start) | copy-done | bytes 131096
  1.5 0.0 copy-start.1
  1.5 0.9 %copy-done.1 = f32[1,32,8,128]{3,2,1,0:T(8,128)S(1)} copy-done((f32[1,32,8,128]{3,2,1,0:T(8,128)S(1)}, f32[1,32,8,128]{3,2,1,0:T(8,128)}, u32[]{:S(2)}) %copy-start.1) | copy-done | bytes 131096
  2.4 0.0 copy-start.2
  2.4 0.9 %copy-done.2 = f32[1,32,8,128]{3,2,1,0:T(8,128)S(1)} copy-done((f32[1,32,8,128]{3,2,1,0:T(8,128)S(1)}, f32[1,32,8,128]{3,2,1,0:T(8,128)}, u32[]{:S(2)}) %copy-start.2) | copy-done | bytes 131096
  3.3 0.0 copy-start.3
  3.3 0.9 %copy-done.3 = f32[1,32,8,128]{3,2,1,0:T(8,128)S(1)} copy-done((f32[1,32,8,128]{3,2,1,0:T(8,128)S(1)}, f32[1,32,8,128]{3,2,1,0:T(8,128)}, u32[]{:S(2)}) %copy-start.3) | copy-done | bytes 131096
  4.3 0.0 copy-start.4
  4.3 0.9 %copy-done.4 = f32[32,8,128]{2,1,0:T(8,128)S(1)} copy-done((f32[32,8,128]{2,1,0:T(8,128)S(1)}, f32[32,8,128]{2,1,0:T(8,128)}, u32[]{:S(2)}) %copy-start.4) | copy-done | bytes 131096
  5.2 0.0 copy-start.5
  5.2 0.7 %copy-done.5 = f32[32,32]{1,0:T(8,128)S(1)} copy-done((f32[32,32]{1,0:T(8,128)S(1)}, f32[32,32]{1,0:T(8,128)}, u32[]{:S(2)}) %copy-start.5) | copy-done | bytes 4120
  5.9 54.1 %shard_map.77 = (f32[1,32,8,128]{3,2,1,0:T(8,128)S(1)}, f32[1,32,8,128]{3,2,1,0:T(8,128)S(1)}) custom-call(f32[1,32,8,128]{3,2,1,0:T(8,128)S(1)} %copy-done, f32[1,32,8,128]{3,2,1,0:T(8,128)S(1)} %copy-done.1, f32[1,32,8,128]{3,2,1,0:T(8,128)S(1)} %copy-done.2, f32[1,32,8,128]{3,2,1,0:T(8,128)S(1)} %copy-done.3, f32[32,8,128]{2,1,0:T(8,128)S(1)} %copy-done.4, ...), custom_call_target="tpu_custom_call" | custom-call | tf_op jit(solution)/shard_map/pallas_call | solution.py:324
  59.9 0.7 %copy.10 = f32[1,32,8,128]{3,2,1,0:T(8,128)} copy(f32[1,32,8,128]{3,2,1,0:T(8,128)S(1)} %get-tuple-element.4) | data formatting | bytes 262144
  60.6 0.7 %copy.11 = f32[1,32,8,128]{3,2,1,0:T(8,128)} copy(f32[1,32,8,128]{3,2,1,0:T(8,128)S(1)} %get-tuple-element.5) | data formatting | bytes 262144
Async XLA Ops:
  0.6 0.9 %copy-start = (f32[1,32,8,128]{3,2,1,0:T(8,128)S(1)}, f32[1,32,8,128]{3,2,1,0:T(8,128)}, u32[]{:S(2)}) copy-start(f32[1,32,8,128]{3,2,1,0:T(8,128)} %st_hbm.1) | copy-start | bytes 393220
  1.5 0.9 %copy-start.1 = (f32[1,32,8,128]{3,2,1,0:T(8,128)S(1)}, f32[1,32,8,128]{3,2,1,0:T(8,128)}, u32[]{:S(2)}) copy-start(f32[1,32,8,128]{3,2,1,0:T(8,128)} %wx_hbm.1) | copy-start | bytes 393220
  2.4 0.9 %copy-start.2 = (f32[1,32,8,128]{3,2,1,0:T(8,128)S(1)}, f32[1,32,8,128]{3,2,1,0:T(8,128)}, u32[]{:S(2)}) copy-start(f32[1,32,8,128]{3,2,1,0:T(8,128)} %wy_hbm.1) | copy-start | bytes 393220
  3.3 0.9 %copy-start.3 = (f32[1,32,8,128]{3,2,1,0:T(8,128)S(1)}, f32[1,32,8,128]{3,2,1,0:T(8,128)}, u32[]{:S(2)}) copy-start(f32[1,32,8,128]{3,2,1,0:T(8,128)} %kf_hbm.1) | copy-start | bytes 393220
  4.3 0.9 %copy-start.4 = (f32[32,8,128]{2,1,0:T(8,128)S(1)}, f32[32,8,128]{2,1,0:T(8,128)}, u32[]{:S(2)}) copy-start(f32[32,8,128]{2,1,0:T(8,128)} %dc_hbm.1) | copy-start | bytes 393220
  5.2 0.7 %copy-start.5 = (f32[32,32]{1,0:T(8,128)S(1)}, f32[32,32]{1,0:T(8,128)}, u32[]{:S(2)}) copy-start(f32[32,32]{1,0:T(8,128)} %tw_ref.1) | copy-start | bytes 12292

commit v2 on v1

--- a/solution.py
+++ b/solution.py
@@ -11,7 +11,7 @@
 
 LEV = 32
 OWN0, OWN1, ROWS = 16, 144, 160
-CHUNK = 16
+CHUNK = 144
 STATE, B, D, K, C = range(5)
 DIRS = ((-1, 0), (1, 0), (-1, -1), (-1, 1), (1, -1), (1, 1), (0, -1), (0, 1))
 
@@ -25,8 +25,7 @@
     low, high = lane < 32, lane >= 96
     lowest, highest = max(first - 1, held), min(last + 1, 5 - held)
 
-    def body(i, carry):
-        row = pl.multiple_of(8 + i * CHUNK, 8)
+    for row in range(8, ROWS - 8, CHUNK):
         here = pl.ds(row, CHUNK)
         v = {p: src[p, here, :] for p in range(lowest, highest + 1)}
         up = {p: rolled(v[p], 32) for p in range(lowest, last + 1)}
@@ -47,17 +46,14 @@
                     + coefs[K, p, here, :] * ((east + north) - (mid + mid))
                 )
             dst[p, here, :] = new
-        return carry
-
-    lax.fori_loop(0, (ROWS - 16) // CHUNK, body, 0)
 
 
 def kernel(
-    st_hbm, wx_hbm, wy_hbm, kf_hbm, dc_hbm, tw_ref,
+    st_hbm, wx_hbm, wy_hbm, kf_hbm, dc_hbm, tw_hbm,
     defect_ref, mixed_ref,
-    raw, ext, second, ping, pong, rows_s, rows_e, rows_o, rows_n, got_s, got_e, prev, dtmp, fin,
+    raw, ext, second, ping, pong, rows_s, rows_e, rows_o, rows_n, got_s, got_e, prev, dtmp, fin, tw_ref,
     load_sem, send1, recv1, send2, recv2, send3, recv3,
-    a2a_send, a2a_recv, next_send, next_recv, out_sem, all_in,
+    a2a_send, a2a_recv, next_send, next_recv, out_sem, all_in, near_in,
 ):
     tm, gx, gy = lax.axis_index("tm"), lax.axis_index("gx"), lax.axis_index("gy")
     ntm, ngx, ngy = lax.axis_size("tm"), lax.axis_size("gx"), lax.axis_size("gy")
@@ -77,20 +73,33 @@
     def neighbour(dx, dy):
         return {"gx": gx + dx, "gy": gy + dy}
 
+    def offset(k):
+        dx, j, c = 1 - k // 16, (k // 2) % 8, 1 - k % 2
+        dy = jnp.where(j % 2 == 0, 4 + j // 2, 4 - (j + 1) // 2)
+        x, y, core = tm // 16, (tm // 2) % 8, tm % 2
+        return ((x + dx) % 2) * 16 + ((y + dy) % 8) * 2 + (core + c) % 2
+
+    def head_at(x, y):
+        odd_x, odd_y = lax.rem(x + 2, 2), lax.rem(y + 2, 2)
+        return 2 * odd_x + 1 - odd_y
+
     barrier = pltpu.get_barrier_semaphore()
+    head = head_at(gx, gy)
+    is_head = tm == head
     for dx, dy in DIRS:
-        @pl.when(there(dx, dy))
+        @pl.when(jnp.logical_and(there(dx, dy), tm != head_at(gx + dx, gy + dy)))
         def _(dx=dx, dy=dy):
             pl.semaphore_signal(barrier, 1, device_id=neighbour(dx, dy), device_id_type=MESH)
 
-    @pl.when(tm > 0)
-    def _():
-        pl.semaphore_signal(barrier, 1, device_id={"tm": 0}, device_id_type=MESH)
+    @pl.when(jnp.logical_not(is_head))
+    def _():
+        pl.semaphore_signal(barrier, 1, device_id={"tm": head}, device_id_type=MESH)
 
     loads = [
         pltpu.make_async_copy(src, raw.at[i], load_sem.at[i])
         for i, src in enumerate((st_hbm.at[0], wx_hbm.at[0], wy_hbm.at[0], kf_hbm.at[0], dc_hbm))
     ]
+    loads.append(pltpu.make_async_copy(tw_hbm, tw_ref, load_sem.at[5]))
     for load in loads:
         load.start()
 
@@ -193,18 +202,31 @@
     count = jnp.int32(0)
     for dx, dy in DIRS:
         count = count + jnp.where(there(dx, dy), 1, 0)
-    pl.semaphore_wait(barrier, count + jnp.where(tm == 0, ntm - 1, 0))
+
+    @pl.when(jnp.logical_not(is_head))
+    def _():
+        pl.semaphore_wait(barrier, count)
+        for dx, dy in DIRS:
+            @pl.when(jnp.logical_and(there(dx, dy), tm == head_at(gx + dx, gy + dy)))
+            def _(dx=dx, dy=dy):
+                pl.semaphore_signal(near_in, 1, device_id=neighbour(dx, dy), device_id_type=MESH)
+
+    @pl.when(is_head)
+    def _():
+        pl.semaphore_wait(near_in, count)
 
     each(copies_first, start)
     each(copies_later, start)
 
-    @pl.when(tm == 0)
-    def _():
-        def tell(i, carry):
-            pl.semaphore_signal(all_in, 1, device_id={"tm": i}, device_id_type=MESH)
+    @pl.when(is_head)
+    def _():
+        pl.semaphore_wait(barrier, ntm - 1)
+
+        def tell(k, carry):
+            pl.semaphore_signal(all_in, 1, device_id={"tm": offset(k)}, device_id_type=MESH)
             return carry
 
-        lax.fori_loop(1, ntm, tell, 0)
+        lax.fori_loop(0, ntm - 1, tell, 0)
 
     each(copies_first, arrived, opposite=True)
 
@@ -216,12 +238,6 @@
         second[p, OWN0:OWN1, :] = pong[p, OWN0:OWN1, :]
     each(copies_second, start)
 
-    def offset(k):
-        dx, j, c = 1 - k // 16, (k // 2) % 8, 1 - k % 2
-        dy = jnp.where(j % 2 == 0, 4 + j // 2, 4 - (j + 1) // 2)
-        x, y, core = tm // 16, (tm // 2) % 8, tm % 2
-        return ((x + dx) % 2) * 16 + ((y + dy) % 8) * 2 + (core + c) % 2
-
     def exchange(n, src_of, dst_of_me):
         def send(k, carry):
             other = offset(k)
@@ -252,7 +268,7 @@
     stencil(ping, pong, ext, 2, 3, True)
     to_rows([pong[p, OWN0:OWN1, :] for p in (2, 3)], rows_s)
 
-    @pl.when(tm > 0)
+    @pl.when(jnp.logical_not(is_head))
     def _():
         pl.semaphore_wait(all_in, 1)
 
@@ -287,6 +303,7 @@
 
     exchanged(0)
     exchanged(1)
+    loads[5].wait()
     weights = tw_ref[...]
     for x in range(8):
         both = got_s[x] - got_e[x, 0:LEV, :]
@@ -317,14 +334,27 @@
     sent(2)
 
 
+def hand_out(a_ref, b_ref, a_out, b_out, held, load_sem, store_sem):
+    parts = [(k, src, dst, pl.ds(16 * h, 16)) for h in range(2) for k, (src, dst) in enumerate(((a_ref, a_out), (b_ref, b_out)))]
+    loads = [pltpu.make_async_copy(src.at[0, p], held.at[k, p], load_sem.at[n]) for n, (k, src, dst, p) in enumerate(parts)]
+    stores = [pltpu.make_async_copy(held.at[k, p], dst.at[0, p], store_sem.at[n]) for n, (k, src, dst, p) in enumerate(parts)]
+    for load in loads:
+        load.start()
+    for load, store in zip(loads, stores):
+        load.wait()
+        store.start()
+    for store in stores:
+        store.wait()
+
+
 def per_device(start_state, wind_x, wind_y, diffusivity, diff_coef, time_weight):
     f32 = jnp.float32
-    any_space = pl.BlockSpec(memory_space=pl.ANY)
+    any_space = pl.BlockSpec(memory_space=pltpu.HBM)
     dma = pltpu.SemaphoreType.DMA
-    return pl.pallas_call(
+    outs = pl.pallas_call(
         kernel,
         out_shape=(jax.ShapeDtypeStruct(start_state.shape, f32),) * 2,
-        in_specs=[any_space] * 5 + [pl.BlockSpec(memory_space=pltpu.VMEM)],
+        in_specs=[any_space] * 6,
         out_specs=(any_space, any_space),
         scratch_shapes=[
             pltpu.VMEM((5, LEV, 8, 128), f32),
@@ -341,16 +371,24 @@
             pltpu.VMEM((8, LEV, 128), f32),
             pltpu.VMEM((LEV, 8, 128), f32),
             pltpu.VMEM((2, 128, 128), f32),
-            dma((5,)),
+            pltpu.VMEM((LEV, LEV), f32),
+            dma((6,)),
             dma((8,)), dma((8,)), dma((8,)), dma((8,)), dma((8,)), dma((8,)),
             dma((3,)), dma((3,)),
             dma, dma, dma,
-            pltpu.SemaphoreType.REGULAR,
+            pltpu.SemaphoreType.REGULAR, pltpu.SemaphoreType.REGULAR,
         ],
         compiler_params=pltpu.CompilerParams(
-            collective_id=0, has_side_effects=True, vmem_limit_bytes=32 * 1024 * 1024
+            collective_id=0, has_side_effects=True, vmem_limit_bytes=62 * 1024 * 1024
         ),
     )(start_state, wind_x, wind_y, diffusivity, diff_coef, time_weight)
+    return pl.pallas_call(
+        hand_out,
+        out_shape=(jax.ShapeDtypeStruct(start_state.shape, f32),) * 2,
+        in_specs=[any_space] * 2,
+        out_specs=(any_space, any_space),
+        scratch_shapes=[pltpu.VMEM((2, LEV, 8, 128), f32), dma((4,)), dma((4,))],
+    )(*outs)
 
 
 def solution(mesh):

time: 61.5 us -> 49.2 us (0.80)
  the two profiles are of different devices: /device:TPU:256 before, /device:TPU:259 now
where the time goes in v2:
time: 49.2 us; the launch traced here: 49 us
  Pallas kernels  48.3 us (98%)
  between operations  0.64 us (1%)
    pallas_call x1, Pallas kernels, per_device(): pl.pallas_call(kernel, out_shape=(jax.ShapeDtypeStruct(start_state.shape,...  46.7 us
    pallas_call x1, Pallas kernels, per_device(): pl.pallas_call(hand_out, out_shape=(jax.ShapeDtypeStruct(start_state.shap...  1.63 us

profile of v2, /device:TPU:259, one launch (start us, length us, event | category | flops | bytes accessed | tf_op | source)
XLA Modules:
  0.0 49.0 jit_solution(5104001483499103048)
XLA Ops:
  0.6 46.7 %shard_map.77 = (f32[1,32,8,128]{3,2,1,0:T(8,128)}, f32[1,32,8,128]{3,2,1,0:T(8,128)}) custom-call(f32[1,32,8,128]{3,2,1,0:T(8,128)} %st_hbm.1, f32[1,32,8,128]{3,2,1,0:T(8,128)} %wx_hbm.1, f32[1,32,8,128]{3,2,1,0:T(8,128)} %wy_hbm.1, f32[1,32,8,128]{3,2,1,0:T(8,128)} %kf_hbm.1, f32[32,8,128]{2,1,0:T(8,128)} %dc_hbm.1, f32[32,32]{1,0:T(8,128)} %tw_hbm.1), custom_call_target="tpu_custom_call" | custom-call | tf_op jit(solution)/shard_map/pallas_call | solution.py:354
  47.4 1.6 %shard_map.78 = (f32[1,32,8,128]{3,2,1,0:T(8,128)}, f32[1,32,8,128]{3,2,1,0:T(8,128)}) custom-call(f32[1,32,8,128]{3,2,1,0:T(8,128)} %get-tuple-element.4.a_ref, f32[1,32,8,128]{3,2,1,0:T(8,128)} %get-tuple-element.5.b_ref), custom_call_target="tpu_custom_call" | custom-call | tf_op jit(solution)/shard_map/pallas_call | solution.py:385

commit v3 on v2

--- a/solution.py
+++ b/solution.py
@@ -75,9 +75,10 @@
 
     def offset(k):
         dx, j, c = 1 - k // 16, (k // 2) % 8, 1 - k % 2
-        dy = jnp.where(j % 2 == 0, 4 + j // 2, 4 - (j + 1) // 2)
-        x, y, core = tm // 16, (tm // 2) % 8, tm % 2
-        return ((x + dx) % 2) * 16 + ((y + dy) % 8) * 2 + (core + c) % 2
+        dy = (4 + j // 2 if j % 2 == 0 else 4 - (j + 1) // 2) if isinstance(k, int) else jnp.where(lax.rem(j, 2) == 0, 4 + j // 2, 4 - (j + 1) // 2)
+        y, core = lax.rem(lax.div(tm, 2), 8), lax.rem(tm, 2)
+        base = tm - 2 * y - core
+        return (base if isinstance(dx, int) and dx == 0 else lax.rem(base + 16 * dx, 32)) + 2 * lax.rem(y + dy, 8) + lax.rem(core + c, 2)
 
     def head_at(x, y):
         odd_x, odd_y = lax.rem(x + 2, 2), lax.rem(y + 2, 2)
@@ -246,7 +247,8 @@
             ).start()
             return carry
 
-        lax.fori_loop(0, ntm - 1, send, 0)
+        for k in range(ntm - 1):
+            send(k, 0)
         pltpu.make_async_copy(src_of(tm), dst_of_me, a2a_recv.at[n]).start()
 
     def exchanged(n):

time: 49.2 us -> 49 us (level)
  no operation moved by 1% of the time
where the time goes in v3:
time: 49 us; the launch traced here: 48.8 us
  Pallas kernels  48.1 us (98%)
  between operations  0.64 us (1%)
    pallas_call x1, Pallas kernels, per_device(): pl.pallas_call(kernel, out_shape=(jax.ShapeDtypeStruct(start_state.shape,...  46.5 us
    pallas_call x1, Pallas kernels, per_device(): pl.pallas_call(hand_out, out_shape=(jax.ShapeDtypeStruct(start_state.shap...  1.63 us

profile of v3, /device:TPU:259, one launch (start us, length us, event | category | flops | bytes accessed | tf_op | source)
XLA Modules:
  0.0 48.8 jit_solution(224284315175531398)
XLA Ops:
  0.6 46.5 %shard_map.77 = (f32[1,32,8,128]{3,2,1,0:T(8,128)}, f32[1,32,8,128]{3,2,1,0:T(8,128)}) custom-call(f32[1,32,8,128]{3,2,1,0:T(8,128)} %st_hbm.1, f32[1,32,8,128]{3,2,1,0:T(8,128)} %wx_hbm.1, f32[1,32,8,128]{3,2,1,0:T(8,128)} %wy_hbm.1, f32[1,32,8,128]{3,2,1,0:T(8,128)} %kf_hbm.1, f32[32,8,128]{2,1,0:T(8,128)} %dc_hbm.1, f32[32,32]{1,0:T(8,128)} %tw_hbm.1), custom_call_target="tpu_custom_call" | custom-call | tf_op jit(solution)/shard_map/pallas_call | solution.py:356
  47.1 1.6 %shard_map.78 = (f32[1,32,8,128]{3,2,1,0:T(8,128)}, f32[1,32,8,128]{3,2,1,0:T(8,128)}) custom-call(f32[1,32,8,128]{3,2,1,0:T(8,128)} %get-tuple-element.4.a_ref, f32[1,32,8,128]{3,2,1,0:T(8,128)} %get-tuple-element.5.b_ref), custom_call_target="tpu_custom_call" | custom-call | tf_op jit(solution)/shard_map/pallas_call | solution.py:387

commit v4 on v3

--- a/solution.py
+++ b/solution.py
@@ -140,10 +140,6 @@
         put(K, half, kf)
         put(B, half, [a + b for a, b in zip(own_rows(1, half), kf)])
         put(D, half, [a + b for a, b in zip(own_rows(2, half), kf)])
-    loads[4].wait()
-    for half in range(2):
-        put(C, half, own_rows(4, half))
-
     def y_slices(dy):
         if dy < 0:
             return pl.ds(OWN0, 8), pl.ds(OWN1, 8)
@@ -160,25 +156,26 @@
     def copies_first(n, dx, dy):
         ys, yd = y_slices(dy)
         if dx == 0:
-            src, dst = ext.at[:, pl.ds(2, 2), ys, :], ext.at[:, pl.ds(2, 2), yd, :]
+            src, dst = ext.at[pl.ds(0, 4), pl.ds(2, 2), ys, :], ext.at[pl.ds(0, 4), pl.ds(2, 2), yd, :]
         else:
             ps, pd = near(dx)
-            arrays = pl.ds(0, 4 if dy == 0 else 5)
+            arrays = pl.ds(0, 4)
             src, dst = ext.at[arrays, ps, ys, :], ext.at[arrays, pd, yd, :]
         return [pltpu.make_async_remote_copy(src, dst, send1.at[n], recv1.at[n], device_id=neighbour(dx, dy), device_id_type=MESH)]
 
     def copies_later(n, dx, dy):
+        ys, yd = y_slices(dy)
+        where = neighbour(dx, dy)
         if dx == 0:
-            return []
-        ys, yd = y_slices(dy)
-        out = []
-        if dy == 0:
+            ps, pd = pl.ds(2, 2), pl.ds(2, 2)
+        else:
             ps, pd = near(dx)
+        out = [pltpu.make_async_remote_copy(
+            ext.at[C, ps, ys, :], ext.at[C, pd, yd, :], send2.at[8 + n], recv2.at[8 + n], device_id=where, device_id_type=MESH)]
+        if dx != 0:
+            ps, pd = far(dx)
             out.append(pltpu.make_async_remote_copy(
-                ext.at[C, ps, ys, :], ext.at[C, pd, yd, :], send2.at[6 + n], recv2.at[6 + n], device_id=neighbour(dx, dy), device_id_type=MESH))
-        ps, pd = far(dx)
-        out.append(pltpu.make_async_remote_copy(
-            ext.at[pl.ds(1, 3), ps, ys, :], ext.at[pl.ds(1, 3), pd, yd, :], send2.at[n], recv2.at[n], device_id=neighbour(dx, dy), device_id_type=MESH))
+                ext.at[pl.ds(1, 3), ps, ys, :], ext.at[pl.ds(1, 3), pd, yd, :], send2.at[n], recv2.at[n], device_id=where, device_id_type=MESH))
         return out
 
     def copies_second(n, dx, dy):
@@ -217,6 +214,9 @@
         pl.semaphore_wait(near_in, count)
 
     each(copies_first, start)
+    loads[4].wait()
+    for half in range(2):
+        put(C, half, own_rows(4, half))
     each(copies_later, start)
 
     @pl.when(is_head)
@@ -375,7 +375,7 @@
             pltpu.VMEM((2, 128, 128), f32),
             pltpu.VMEM((LEV, LEV), f32),
             dma((6,)),
-            dma((8,)), dma((8,)), dma((8,)), dma((8,)), dma((8,)), dma((8,)),
+            dma((8,)), dma((8,)), dma((16,)), dma((16,)), dma((8,)), dma((8,)),
             dma((3,)), dma((3,)),
             dma, dma, dma,
             pltpu.SemaphoreType.REGULAR, pltpu.SemaphoreType.REGULAR,

time: 49 us -> 49.1 us (level)
  no operation moved by 1% of the time
where the time goes in v4:
time: 49.1 us; the launch traced here: 48.9 us
  Pallas kernels  48.2 us (98%)
  between operations  0.64 us (1%)
    pallas_call x1, Pallas kernels, per_device(): pl.pallas_call(kernel, out_shape=(jax.ShapeDtypeStruct(start_state.shape,...  46.6 us
    pallas_call x1, Pallas kernels, per_device(): pl.pallas_call(hand_out, out_shape=(jax.ShapeDtypeStruct(start_state.shap...  1.63 us

profile of v4, /device:TPU:259, one launch (start us, length us, event | category | flops | bytes accessed | tf_op | source)
XLA Modules:
  0.0 48.9 jit_solution(8478128709061099948)
XLA Ops:
  0.6 46.6 %shard_map.77 = (f32[1,32,8,128]{3,2,1,0:T(8,128)}, f32[1,32,8,128]{3,2,1,0:T(8,128)}) custom-call(f32[1,32,8,128]{3,2,1,0:T(8,128)} %st_hbm.1, f32[1,32,8,128]{3,2,1,0:T(8,128)} %wx_hbm.1, f32[1,32,8,128]{3,2,1,0:T(8,128)} %wy_hbm.1, f32[1,32,8,128]{3,2,1,0:T(8,128)} %kf_hbm.1, f32[32,8,128]{2,1,0:T(8,128)} %dc_hbm.1, f32[32,32]{1,0:T(8,128)} %tw_hbm.1), custom_call_target="tpu_custom_call" | custom-call | tf_op jit(solution)/shard_map/pallas_call | solution.py:356
  47.2 1.6 %shard_map.78 = (f32[1,32,8,128]{3,2,1,0:T(8,128)}, f32[1,32,8,128]{3,2,1,0:T(8,128)}) custom-call(f32[1,32,8,128]{3,2,1,0:T(8,128)} %get-tuple-element.4.a_ref, f32[1,32,8,128]{3,2,1,0:T(8,128)} %get-tuple-element.5.b_ref), custom_call_target="tpu_custom_call" | custom-call | tf_op jit(solution)/shard_map/pallas_call | solution.py:387
